TPU v7x, 32 devices: a whole 2x2x4 slice. The times are simulated.
32 devices in a mesh: ctx: 8 (over z, x), grp: 4 (over y, core).
Axes of the slice: x: 2, y: 2, z: 4, core: 2. Of those that a mesh axis runs over, the one named last changes fastest.
Arguments:
- queries: bfloat16 [5120, 4096], P(('ctx', 'grp')), may hold values from -27 to 27
- keys: bfloat16 [5120, 512], P(('ctx', 'grp')), may hold values from -4.5 to 4.5
- values: bfloat16 [5120, 512], P(('ctx', 'grp')), may hold values from -6 to 6
- lengths: int32 [16], replicated, may hold values from 1 to 640, 5120 in all
- ssmax_scale: float32 [32], replicated, may hold values from 0.3 to 0.9
Outputs:
- attended: bfloat16 [5120, 4096], P(('ctx', 'grp'))
Inputs may be any that keep to these rules, and one draw needn't show every extreme that they name: Every document has 1 to 640 tokens and one has exactly 640; the lengths sum to 5120.
All inputs are finite; a program needn't handle non-finite values.
Results may differ from a plain program's by a relative error of at most 0.0047.
Values may be sent and summed in bfloat16 or wider, within the bound.
A program may use at most 64 MiB of HBM per device.

v0:
```python
import jax
import jax.numpy as jnp
from jax import lax
from jax.sharding import PartitionSpec as P

HQ = 32
HK = 4
HD = 128
WIN_DEV = 4


def from_behind(x, axis, by):
    count = lax.axis_size(axis)
    pairs = [(i, i + by) for i in range(count) if 0 <= i + by < count]
    return lax.ppermute(x, axis, pairs)


def body(queries, keys, values, lengths, ssmax_scale):
    tok_rows = queries.shape[0]
    slab_rows = tok_rows * lax.axis_size("grp")
    doc_most = WIN_DEV * tok_rows
    win_width = doc_most + tok_rows
    per_group = HQ // HK
    grp_index = lax.axis_index("grp")
    ctx_index = lax.axis_index("ctx")
    q_start = ctx_index * slab_rows + grp_index * tok_rows
    q_pos = q_start + jnp.arange(tok_rows, dtype=jnp.int32)
    own_keys, own_values = (
        lax.all_gather(keys, "grp", axis=0, tiled=True),
        lax.all_gather(values, "grp", axis=0, tiled=True),
    )
    prior_keys, prior_values = from_behind((own_keys, own_values), "ctx", 1)
    joined_keys = jnp.concatenate([prior_keys, own_keys], axis=0)
    joined_values = jnp.concatenate([prior_values, own_values], axis=0)
    win_begin = slab_rows + grp_index * tok_rows - doc_most
    k_window = lax.dynamic_slice_in_dim(joined_keys, win_begin, win_width, 0)
    v_window = lax.dynamic_slice_in_dim(joined_values, win_begin, win_width, 0)
    k_pos = ctx_index * slab_rows - slab_rows + win_begin + jnp.arange(win_width, dtype=jnp.int32)
    totals = jnp.cumsum(lengths, dtype=jnp.int32)
    before = totals[None, :] <= q_pos[:, None]
    doc_start = jnp.sum(jnp.where(before, lengths[None, :], 0), axis=1, dtype=jnp.int32)
    visible = (q_pos - doc_start + 1).astype(jnp.float32)
    score_coef = ssmax_scale[None, :] * jnp.log(visible)[:, None] / jnp.sqrt(jnp.float32(HD))
    live_mask = (k_pos[None, :] >= doc_start[:, None]) & (k_pos[None, :] <= q_pos[:, None])
    pieces = []
    for kv_head in range(HK):
        q_heads = queries[:, kv_head * per_group * HD : (kv_head + 1) * per_group * HD].reshape(
            tok_rows, per_group, HD
        )
        k_head = k_window[:, kv_head * HD : (kv_head + 1) * HD]
        v_head = v_window[:, kv_head * HD : (kv_head + 1) * HD]
        head_coef = score_coef[:, kv_head * per_group : (kv_head + 1) * per_group].T[:, :, None]
        scores = (
            jnp.einsum("igd,jd->gij", q_heads, k_head, preferred_element_type=jnp.float32)
            * head_coef
        )
        scores = jnp.where(live_mask[None], scores, -jnp.inf)
        top_score = jnp.max(scores, axis=-1, keepdims=True)
        probs = jnp.exp(scores - top_score)
        weights = (probs / jnp.sum(probs, axis=-1, keepdims=True)).astype(jnp.bfloat16)
        mixed = jnp.einsum("gij,jd->igd", weights, v_head, preferred_element_type=jnp.float32)
        pieces.append(mixed.reshape(tok_rows, per_group * HD))
    return jnp.concatenate(pieces, axis=1).astype(jnp.bfloat16)


def solution(mesh):
    return jax.shard_map(
        body,
        mesh=mesh,
        in_specs=(
            P(("ctx", "grp"), None),
            P(("ctx", "grp"), None),
            P(("ctx", "grp"), None),
            P(),
            P(),
        ),
        out_specs=P(("ctx", "grp"), None),
        check_vma=False,
    )
```

profile of v0, /device:TPU:24, one launch (start us, length us, event | category | flops | bytes accessed | tf_op | source)
XLA Modules:
  0.0 74.5 jit_solution(847223042924167406)
XLA Ops:
  0.0 8.1 %all_gather.6 = bf16[640,512]{1,0:T(8,128)(2,1)S(1)} all-gather(bf16[160,512]{1,0:T(8,128)(2,1)} %param.7), channel_id=1, replica_groups=mesh['ctx'=8,'grp'=4] {'grp'}, dimensions={0}, use_global_device_ids=true | all-gather | bytes 819200 | tf_op jit(solution)/shard_map/all_gather | solution.py:30
  8.1 3.4 %collective-permute-start = (bf16[640,512]{1,0:T(8,128)(2,1)S(1)}, bf16[640,512]{1,0:T(8,128)(2,1)S(1)}, u32[]{:S(2)}, u32[]{:S(2)}) collective-permute-start(bf16[640,512]{1,0:T(8,128)(2,1)S(1)} %all_gather.6), channel_id=1, source_target_pairs={{0,4},{4,8},{8,12},{12,16},{16,20},{20,24},{24,28},{1,5},{5,9},{9,... | collective-permute-start | bytes 1966088 | tf_op jit(solution)/shard_map/ppermute | solution.py:15
  11.5 7.9 %all_gather.7 = bf16[640,512]{1,0:T(8,128)(2,1)S(1)} all-gather(bf16[160,512]{1,0:T(8,128)(2,1)} %param.6), channel_id=1, replica_groups=mesh['ctx'=8,'grp'=4] {'grp'}, dimensions={0}, use_global_device_ids=true | all-gather | bytes 819200 | tf_op jit(solution)/shard_map/all_gather | solution.py:29
  19.4 1.9 %collective-permute-start.1 = (bf16[640,512]{1,0:T(8,128)(2,1)S(1)}, bf16[640,512]{1,0:T(8,128)(2,1)}, u32[]{:S(2)}, u32[]{:S(2)}) collective-permute-start(bf16[640,512]{1,0:T(8,128)(2,1)S(1)} %all_gather.7), channel_id=1, source_target_pairs={{0,4},{4,8},{8,12},{12,16},{16,20},{20,24},{24,28},{1,5},{5,9},{9,... | collective-permute-start | bytes 1966088 | tf_op jit(solution)/shard_map/ppermute | solution.py:15
  21.4 0.7 copy.16
  22.2 0.1 reduce
  22.3 0.7 select_reduce_fusion
  23.0 0.7 multiply_multiply_fusion
  23.8 0.2 compare_and_fusion
  24.0 2.2 %slice_bitcast_fusion.3 = (bf16[20,8,8,128]{3,2,1,0:T(8,128)(2,1)}, bf16[20,8,8,128]{3,2,1,0:T(8,128)(2,1)}, bf16[20,8,8,128]{3,2,1,0:T(8,128)(2,1)}, bf16[20,8,8,128]{3,2,1,0:T(8,128)(2,1)S(1)}) fusion(bf16[160,4096]{1,0:T(8,128)(2,1)} %param.5), kind=kLoop, calls=%fused_computation.79 | loop fusion | bytes 2621440
  26.2 2.2 %collective-permute-done = bf16[640,512]{1,0:T(8,128)(2,1)S(1)} collective-permute-done((bf16[640,512]{1,0:T(8,128)(2,1)S(1)}, bf16[640,512]{1,0:T(8,128)(2,1)S(1)}, u32[]{:S(2)}, u32[]{:S(2)}) %collective-permute-start) | collective-permute-done | bytes 655392 | tf_op jit(solution)/shard_map/ppermute | solution.py:15
  28.4 0.0 copy-start
  28.4 0.8 %copy-done = bf16[640,512]{1,0:T(8,128)(2,1)} copy-done((bf16[640,512]{1,0:T(8,128)(2,1)}, bf16[640,512]{1,0:T(8,128)(2,1)S(1)}, u32[]{:S(2)}) %copy-start) | copy-done | bytes 655384
  29.3 12.7 %collective-permute-done.1 = bf16[640,512]{1,0:T(8,128)(2,1)} collective-permute-done((bf16[640,512]{1,0:T(8,128)(2,1)S(1)}, bf16[640,512]{1,0:T(8,128)(2,1)}, u32[]{:S(2)}, u32[]{:S(2)}) %collective-permute-start.1) | collective-permute-done | bytes 655392 | tf_op jit(solution)/shard_map/ppermute | solution.py:15
  42.0 2.3 %fusion.48 = (bf16[800,512]{1,0:T(8,128)(2,1)S(1)}, bf16[800,512]{1,0:T(8,128)(2,1)S(1)}) fusion(s32[]{:T(128)S(6)} %select_n.21, bf16[640,512]{1,0:T(8,128)(2,1)} %collective-permute-done.1, bf16[640,512]{1,0:T(8,128)(2,1)S(1)} %all_gather.7, bf16[640,512]{1,0:T(8,128)(2,1)S(1)} %all_gather.6, bf16[640,512]{1,0:T(8,128)(2,1)} %copy-done), kind=kLoop, calls=%fused_computation.53 | loop fusion | flops 3276800 | bytes 4259844 | tf_op jit(solution)/shard_map/concatenate | solution.py:33
  44.3 4.8 %fusion.121 = (f32[8,160]{1,0:T(8,128)S(1)}, f32[8,160,800]{2,1,0:T(8,128)}) fusion(f32[8,160]{1,0:T(8,128)S(1)} %get-tuple-element.9, pred[160,800]{1,0:T(8,128)(4,1)S(1)} %compare_and_fusion, bf16[20,8,8,128]{3,2,1,0:T(8,128)(2,1)} %get-tuple-element.5, bf16[800,512]{1,0:T(8,128)(2,1)S(1)} %get-tuple-element.21), kind=kOutput, calls=%fused_computation.112 | convolution fusion | flops 266240800 | bytes 4785152 | tf_op jit(solution)/shard_map/sub | solution.py:59
  49.1 0.0 copy-start.2
  49.1 3.2 %fusion.44 = bf16[8,20,8,128]{3,2,1,0:T(8,128)(2,1)S(1)} fusion(f32[8,160,800]{2,1,0:T(8,128)} %get-tuple-element.20, f32[8,160]{1,0:T(8,128)S(1)} %get-tuple-element.19, bf16[800,512]{1,0:T(8,128)(2,1)S(1)} %get-tuple-element.22), kind=kOutput, calls=%fused_computation.49 | convolution fusion | flops 264355840 | bytes 4636672 | tf_op jit(solution)/shard_map/gij,jd->igd/dot_general | solution.py:61
  52.2 0.1 copy.104
  52.3 0.0 copy-done.2
  52.3 3.8 %fusion.116 = (f32[8,160]{1,0:T(8,128)S(1)}, f32[8,160,800]{2,1,0:T(8,128)}) fusion(f32[8,160]{1,0:T(8,128)S(1)} %get-tuple-element.12, pred[160,800]{1,0:T(8,128)(4,1)S(1)} %compare_and_fusion, bf16[20,8,8,128]{3,2,1,0:T(8,128)(2,1)S(1)} %copy-done.2, bf16[800,512]{1,0:T(8,128)(2,1)S(1)} %get-tuple-element.21), kind=kOutput, calls=%fused_computation.111 | convolution fusion | flops 266240800 | bytes 4785152 | tf_op jit(solution)/shard_map/sub | solution.py:59
  56.1 0.0 copy-start.1
  56.1 3.2 %fusion.45 = bf16[8,20,8,128]{3,2,1,0:T(8,128)(2,1)S(1)} fusion(f32[8,160,800]{2,1,0:T(8,128)} %get-tuple-element.18, f32[8,160]{1,0:T(8,128)S(1)} %get-tuple-element.17, bf16[800,512]{1,0:T(8,128)(2,1)S(1)} %get-tuple-element.22), kind=kOutput, calls=%fused_computation.50 | convolution fusion | flops 264355840 | bytes 4636672 | tf_op jit(solution)/shard_map/gij,jd->igd/dot_general | solution.py:61
  59.3 0.1 copy.103
  59.4 0.0 copy-done.1
  59.4 3.8 %fusion.106 = (f32[8,160]{1,0:T(8,128)S(1)}, f32[8,160,800]{2,1,0:T(8,128)}) fusion(f32[8,160]{1,0:T(8,128)S(1)} %get-tuple-element.10, pred[160,800]{1,0:T(8,128)(4,1)S(1)} %compare_and_fusion, bf16[20,8,8,128]{3,2,1,0:T(8,128)(2,1)S(1)} %copy-done.1, bf16[800,512]{1,0:T(8,128)(2,1)S(1)} %get-tuple-element.21), kind=kOutput, calls=%fused_computation.109 | convolution fusion | flops 266240800 | bytes 4785152 | tf_op jit(solution)/shard_map/sub | solution.py:59
  63.2 3.1 %fusion.47 = bf16[8,20,8,128]{3,2,1,0:T(8,128)(2,1)S(1)} fusion(f32[8,160,800]{2,1,0:T(8,128)} %get-tuple-element.14, f32[8,160]{1,0:T(8,128)S(1)} %get-tuple-element.13, bf16[800,512]{1,0:T(8,128)(2,1)S(1)} %get-tuple-element.22), kind=kOutput, calls=%fused_computation.52 | convolution fusion | flops 264355840 | bytes 4636672 | tf_op jit(solution)/shard_map/gij,jd->igd/dot_general | solution.py:61
  66.3 0.1 copy.101
  66.4 3.8 %fusion.111 = (f32[8,160]{1,0:T(8,128)S(1)}, f32[8,160,800]{2,1,0:T(8,128)}) fusion(f32[8,160]{1,0:T(8,128)S(1)} %get-tuple-element.11, pred[160,800]{1,0:T(8,128)(4,1)S(1)} %compare_and_fusion, bf16[20,8,8,128]{3,2,1,0:T(8,128)(2,1)S(1)} %get-tuple-element.8, bf16[800,512]{1,0:T(8,128)(2,1)S(1)} %get-tuple-element.21), kind=kOutput, calls=%fused_computation.110 | convolution fusion | flops 266240800 | bytes 4785152 | tf_op jit(solution)/shard_map/sub | solution.py:59
  70.1 3.1 %fusion.46 = bf16[8,20,8,128]{3,2,1,0:T(8,128)(2,1)S(1)} fusion(f32[8,160,800]{2,1,0:T(8,128)} %get-tuple-element.16, f32[8,160]{1,0:T(8,128)S(1)} %get-tuple-element.15, bf16[800,512]{1,0:T(8,128)(2,1)S(1)} %get-tuple-element.22), kind=kOutput, calls=%fused_computation.51 | convolution fusion | flops 264355840 | bytes 4636672 | tf_op jit(solution)/shard_map/gij,jd->igd/dot_general | solution.py:61
  73.3 0.1 copy.102
  73.4 1.2 %pad_maximum_fusion = bf16[160,4096]{1,0:T(8,128)(2,1)} fusion(bf16[160,1024]{1,0:T(8,128)(2,1)S(1)} %bitcast.199, bf16[160,1024]{1,0:T(8,128)(2,1)S(1)} %bitcast.200, bf16[160,1024]{1,0:T(8,128)(2,1)S(1)} %bitcast.198, bf16[160,1024]{1,0:T(8,128)(2,1)S(1)} %bitcast.197), kind=kLoop, calls=%fused_computation.44 | loop fusion | flops 5242880 | bytes 2621440 | tf_op jit(solution)/shard_map/concatenate | solution.py:63
  (5 shorter events, 0.1 us)
Async XLA Ops:
  8.1 20.3 %collective-permute-start = (bf16[640,512]{1,0:T(8,128)(2,1)S(1)}, bf16[640,512]{1,0:T(8,128)(2,1)S(1)}, u32[]{:S(2)}, u32[]{:S(2)}) collective-permute-start(bf16[640,512]{1,0:T(8,128)(2,1)S(1)} %all_gather.6), channel_id=1, source_target_pairs={{0,4},{4,8},{8,12},{12,16},{16,20},{20,24},{24,28},{1,5},{5,9},{9,... | collective-permute-start | bytes 1966088 | tf_op jit(solution)/shard_map/ppermute | solution.py:15
  19.4 22.6 %collective-permute-start.1 = (bf16[640,512]{1,0:T(8,128)(2,1)S(1)}, bf16[640,512]{1,0:T(8,128)(2,1)}, u32[]{:S(2)}, u32[]{:S(2)}) collective-permute-start(bf16[640,512]{1,0:T(8,128)(2,1)S(1)} %all_gather.7), channel_id=1, source_target_pairs={{0,4},{4,8},{8,12},{12,16},{16,20},{20,24},{24,28},{1,5},{5,9},{9,... | collective-permute-start | bytes 1966088 | tf_op jit(solution)/shard_map/ppermute | solution.py:15
  28.4 0.8 %copy-start = (bf16[640,512]{1,0:T(8,128)(2,1)}, bf16[640,512]{1,0:T(8,128)(2,1)S(1)}, u32[]{:S(2)}) copy-start(bf16[640,512]{1,0:T(8,128)(2,1)S(1)} %collective-permute-done) | copy-start | bytes 1966084
  49.1 3.3 %copy-start.2 = (bf16[20,8,8,128]{3,2,1,0:T(8,128)(2,1)S(1)}, bf16[20,8,8,128]{3,2,1,0:T(8,128)(2,1)}, u32[]{:S(2)}) copy-start(bf16[20,8,8,128]{3,2,1,0:T(8,128)(2,1)} %get-tuple-element.6) | copy-start | bytes 983044
  56.1 3.3 %copy-start.1 = (bf16[20,8,8,128]{3,2,1,0:T(8,128)(2,1)S(1)}, bf16[20,8,8,128]{3,2,1,0:T(8,128)(2,1)}, u32[]{:S(2)}) copy-start(bf16[20,8,8,128]{3,2,1,0:T(8,128)(2,1)} %get-tuple-element.7) | copy-start | bytes 983044
where the time goes:
time: 74.9 us; the launch traced here: 74.5 us
  matrix products  28.6 us (38%)
  blocking collectives  16 us (21%)
  waiting for transfers between devices  15 us (20%)
  starting transfers between devices  5.3 us (7%)
  other arithmetic  5.26 us (7%)
  local copies, waits for them, and re-layouts  4.14 us (6%)
    sub x4, matrix products, body(): probs = jnp.exp(scores - top_score)  16.1 us
    ppermute x2, waiting for transfers between devices, from_behind(): return lax.ppermute(x, axis, pairs)  15 us
    dot_general x4, matrix products, body(): jnp.einsum('gij,jd->igd', weights, v_head, preferred_element_type=jnp.flo...  12.5 us
    all_gather x1, blocking collectives, body(): lax.all_gather(values, 'grp', axis=0, tiled=True)  8.11 us
    all_gather x1, blocking collectives, body(): lax.all_gather(keys, 'grp', axis=0, tiled=True)  7.94 us
    ppermute x2, starting transfers between devices, from_behind(): return lax.ppermute(x, axis, pairs)  5.3 us
    unnamed x7, local copies, waits for them, and re-layouts  3.09 us
    concatenate x1, other arithmetic, body(): joined_keys = jnp.concatenate([prior_keys, own_keys], axis=0)  2.28 us
  transfers between devices with their start and end apart: 2, of which 2 were waited for; matrix products, arithmetic and copies ran while one was open for 6% of the time, Pallas kernels for 0%

commit v1 on v0

v1 whole, which is shorter than its diff:
```python
import functools
import math

import jax
import jax.numpy as jnp
from jax import lax
from jax.experimental import pallas as pl
from jax.experimental.pallas import tpu as pltpu
from jax.sharding import PartitionSpec as P

HQ = 32
HK = 4
HD = 128
WIN_DEV = 4
PER = HQ // HK
HALVES = 2
HALF = HK * HD // HALVES
MESH = pl.DeviceIdType.MESH
MASKED = -1e30


def kernel(
    n_ctx, n_grp, scale_ref, len_ref, q_ref, k_ref, v_ref, o_ref,
    kw, vw, bias_own, bias_win, lv, acc, top, send_sem, recv_sem,
):
    rows = q_ref.shape[0]
    n_dev = n_ctx * n_grp
    c = lax.axis_index("ctx")
    g = lax.axis_index("grp")
    me = c * n_grp + g
    core = lax.rem(g, 2)
    relay = n_grp == 4

    def at(lin):
        return (lin // n_grp, lin % n_grp)

    sibling = (c, g + 1 - 2 * core)
    across = (c, lax.rem(g + 2, 4))

    barrier = pltpu.get_barrier_semaphore()

    def greet(dev):
        pl.semaphore_signal(barrier, inc=1, device_id=dev, device_id_type=MESH)

    has4, to4 = me >= 4, me + 4 < n_dev
    has2, to2 = me >= 2, me + 2 < n_dev
    greet(sibling)
    count = 1 + has4.astype(jnp.int32) + to4.astype(jnp.int32)

    @pl.when(has4)
    def _():
        greet(at(me - 4))

    @pl.when(to4)
    def _():
        greet(at(me + 4))

    if relay:
        greet(across)
        count = count + 1
    else:
        count = count + has2.astype(jnp.int32) + to2.astype(jnp.int32)

        @pl.when(has2)
        def _():
            greet(at(me - 2))

        @pl.when(to2)
        def _():
            greet(at(me + 2))

    @pl.when(jnp.logical_not(has4))
    def _():
        kw[0] = jnp.zeros(kw.shape[1:], kw.dtype)
        vw[0] = jnp.zeros(vw.shape[1:], vw.dtype)

    if not relay:

        @pl.when(jnp.logical_not(has2))
        def _():
            kw[2] = jnp.zeros(kw.shape[1:], kw.dtype)
            vw[2] = jnp.zeros(vw.shape[1:], vw.dtype)

    pl.semaphore_wait(barrier, count)

    def copies(src_slot, dst_slot, kind, half, dev):
        cols = pl.ds(half * HALF, HALF)
        made = []
        for i, (own, win) in enumerate(((k_ref, kw), (v_ref, vw))):
            src = own.at[:, cols] if src_slot is None else win.at[src_slot, :, cols]
            made.append(
                pltpu.make_async_remote_copy(
                    src_ref=src,
                    dst_ref=win.at[dst_slot, :, cols],
                    send_sem=send_sem.at[kind, half, i],
                    recv_sem=recv_sem.at[dst_slot, half, i],
                    device_id=dev,
                    device_id_type=MESH,
                )
            )
        return made

    def start(*args):
        for copy in copies(*args):
            copy.start()

    def arrived(slot, half):
        for copy in copies(None, slot, 0, half, sibling):
            copy.wait_recv()

    def sent(kind, half):
        for copy in copies(None, 0, kind, half, sibling):
            copy.wait_send()

    first_chip = g < 2
    for half in range(HALVES):

        @pl.when(to4)
        def _(half=half):
            start(None, 0, 0, half, at(me + 4))

        if relay:

            @pl.when(first_chip)
            def _(half=half):
                start(None, 2, 1, half, across)

        else:

            @pl.when(to2)
            def _(half=half):
                start(None, 2, 1, half, at(me + 2))

        @pl.when(core == 0)
        def _(half=half):
            start(None, 3, 2, half, sibling)

    def pass_on_far(half):
        @pl.when(has4)
        def _():
            arrived(0, half)

        if relay:

            @pl.when(jnp.logical_not(first_chip))
            def _():
                start(0, 2, 1, half, across)

        @pl.when(core == 1)
        def _():
            start(0, 1, 2, half, sibling)

    def pass_on_near(half):
        if relay:
            arrived(2, half)
        else:

            @pl.when(has2)
            def _():
                arrived(2, half)

        @pl.when(core == 0)
        def _():
            start(2, 1, 3, half, sibling)

        @pl.when(core == 1)
        def _():
            start(2, 3, 3, half, sibling)

    pos = me * rows + lax.broadcasted_iota(jnp.int32, (rows, HD), 0)

    def doc(j, carry):
        total, begin = carry
        total = total + len_ref[j]
        return total, jnp.where(total <= pos, total, begin)

    _, begin = lax.fori_loop(0, len_ref.shape[0], doc, (jnp.int32(0), jnp.zeros_like(pos)))
    visible = pos - begin + 1
    factor = jnp.log(visible.astype(jnp.float32)) * (math.log2(math.e) / math.sqrt(HD))
    lv[...] = jnp.where(visible == 1, 1.0, factor)
    for ref, base in ((bias_own, me * rows), (bias_win, (me - WIN_DEV) * rows)):
        shape = ref.shape
        k_pos = base + lax.broadcasted_iota(jnp.int32, shape, 1)
        q_pos = me * rows + lax.broadcasted_iota(jnp.int32, shape, 0)
        live = (k_pos >= jnp.broadcast_to(begin[:, :1], shape)) & (k_pos <= q_pos)
        ref[...] = jnp.where(live, 0.0, MASKED)

    def head_cols(h):
        return pl.ds(pl.multiple_of(h * HD, HD), HD)

    def stacked(kv):
        q = jnp.concatenate([q_ref[:, head_cols(kv * PER + i)] for i in range(PER)], axis=0)
        fac = jnp.concatenate([lv[...] * scale_ref[kv * PER + i] for i in range(PER)], axis=0)
        return q, fac[:, :1]

    def scores(q, keys, bias):
        s = lax.dot_general(q, keys, (((1,), (1,)), ((), ())), preferred_element_type=jnp.float32)
        s = s.reshape(PER, rows, bias.shape[1]) + bias[...][None]
        return s.reshape(PER * rows, bias.shape[1])

    def mix(p, vals):
        wide = jnp.concatenate([vals, jnp.ones(vals.shape, vals.dtype)], axis=1)
        return jnp.dot(p.astype(jnp.bfloat16), wide, preferred_element_type=jnp.float32)

    def own_part(kv, _):
        q, fac = stacked(kv)
        s = scores(q, k_ref[:, head_cols(kv)], bias_own)
        m = jnp.max(s, axis=1, keepdims=True)
        acc[kv] = mix(jnp.exp2((s - m) * fac), v_ref[:, head_cols(kv)])
        top[kv] = jnp.broadcast_to(m, top.shape[1:])
        return 0

    def window_part(kv, _):
        q, fac = stacked(kv)
        keys = kw[:, :, head_cols(kv)].reshape(WIN_DEV * rows, HD)
        vals = vw[:, :, head_cols(kv)].reshape(WIN_DEV * rows, HD)
        s = scores(q, keys, bias_win)
        m_own = top[kv][:, :1]
        m = jnp.maximum(m_own, jnp.max(s, axis=1, keepdims=True))
        part = mix(jnp.exp2((s - m) * fac), vals)
        both = acc[kv] * jnp.exp2((m_own - m) * fac) + part
        out = (both[:, :HD] / both[:, HD:]).astype(o_ref.dtype)
        for i in range(PER):
            o_ref[:, head_cols(kv * PER + i)] = out[i * rows : (i + 1) * rows]
        return 0

    per_half = HK // HALVES
    lax.fori_loop(0, per_half, own_part, 0)
    pass_on_far(0)
    lax.fori_loop(per_half, HK, own_part, 0)
    pass_on_near(0)
    pass_on_far(1)
    pass_on_near(1)
    for half in range(HALVES):
        arrived(1, half)
        arrived(3, half)
        lax.fori_loop(half * per_half, (half + 1) * per_half, window_part, 0)

    for half in range(HALVES):

        @pl.when(to4)
        def _(half=half):
            sent(0, half)

        if relay:
            sent(1, half)
        else:

            @pl.when(to2)
            def _(half=half):
                sent(1, half)

        sent(2, half)
        sent(3, half)


def body(queries, keys, values, lengths, ssmax_scale):
    rows = queries.shape[0]
    n_ctx, n_grp = lax.axis_size("ctx"), lax.axis_size("grp")
    vmem = pl.BlockSpec(memory_space=pltpu.VMEM)
    smem = pl.BlockSpec(memory_space=pltpu.SMEM)
    window = pltpu.VMEM((WIN_DEV, rows, HK * HD), jnp.bfloat16)
    pairs = HQ * rows * (WIN_DEV + 1) * rows
    return pl.pallas_call(
        functools.partial(kernel, n_ctx, n_grp),
        out_shape=jax.ShapeDtypeStruct(queries.shape, queries.dtype),
        in_specs=[smem, smem, vmem, vmem, vmem],
        out_specs=vmem,
        scratch_shapes=[
            window,
            window,
            pltpu.VMEM((rows, rows), jnp.float32),
            pltpu.VMEM((rows, WIN_DEV * rows), jnp.float32),
            pltpu.VMEM((rows, HD), jnp.float32),
            pltpu.VMEM((HK, PER * rows, 2 * HD), jnp.float32),
            pltpu.VMEM((HK, PER * rows, HD), jnp.float32),
            pltpu.SemaphoreType.DMA((4, HALVES, 2)),
            pltpu.SemaphoreType.DMA((4, HALVES, 2)),
        ],
        compiler_params=pltpu.CompilerParams(
            collective_id=0, has_side_effects=True, vmem_limit_bytes=48 * 1024 * 1024
        ),
        cost_estimate=pl.CostEstimate(
            flops=4 * pairs * HD, bytes_accessed=4 * queries.size, transcendentals=pairs
        ),
    )(ssmax_scale, lengths, queries, keys, values)


def solution(mesh):
    spec = P(("ctx", "grp"), None)
    return jax.shard_map(
        body,
        mesh=mesh,
        in_specs=(spec, spec, spec, P(), P()),
        out_specs=spec,
        check_vma=False,
    )
```

time: 74.9 us -> 33.9 us (0.45)
  matrix products: 28.6 us -> 0 us
  Pallas kernels: 0 us -> 28.2 us
  blocking collectives: 16 us -> 0 us
  waiting for transfers between devices: 15 us -> 0 us
  starting transfers between devices: 5.3 us -> 0 us
  other arithmetic: 5.26 us -> 0 us
  local copies, waits for them, and re-layouts: 4.14 us -> 5.51 us
    pallas_call x0 -> x1, Pallas kernels: none -> 28.2 us  [body(): pl.pallas_call(functools.partial(kernel, n_ctx, n_grp), out_shape=jax.Sha...]
    sub x4 -> x0, matrix products: 16.1 us -> none  [body(): probs = jnp.exp(scores - top_score)]
    all_gather x2 -> x0, blocking collectives: 16 us -> none  [the longest x1 8.11 us: body(): lax.all_gather(values, 'grp', axis=0, tiled=True)]
    ppermute x2 -> x0, waiting for transfers between devices: 15 us -> none  [from_behind(): return lax.ppermute(x, axis, pairs)]
    dot_general x4 -> x0, matrix products: 12.5 us -> none  [body(): jnp.einsum('gij,jd->igd', weights, v_head, preferred_element_type=jnp.flo...]
    ppermute x2 -> x0, starting transfers between devices: 5.3 us -> none  [from_behind(): return lax.ppermute(x, axis, pairs)]
    concatenate x2 -> x0, other arithmetic: 3.43 us -> none  [the longest x1 2.28 us: body(): joined_keys = jnp.concatenate([prior_keys, own_keys], axis=0)]
    unnamed x7 -> x11, local copies, waits for them, and re-layouts: 3.09 us -> 5.51 us
  transfers between devices with their start and end apart: 2 -> 0, of which waited for: 2 -> 0; matrix products, arithmetic and copies ran while one was open for 6% -> 0% of each run, Pallas kernels for 0% -> 0%
where the time goes in v1:
time: 33.9 us; the launch traced here: 33.7 us
  Pallas kernels  28.2 us (83%)
  local copies, waits for them, and re-layouts  5.51 us (16%)
    pallas_call x1, Pallas kernels, body(): pl.pallas_call(functools.partial(kernel, n_ctx, n_grp), out_shape=jax.Sha...  28.2 us
    unnamed x11, local copies, waits for them, and re-layouts  5.51 us

profile of v1, /device:TPU:24, one launch (start us, length us, event | category | flops | bytes accessed | tf_op | source)
XLA Modules:
  0.0 33.7 jit_solution(15175325587389447176)
XLA Ops:
  0.0 0.0 copy-start
  0.0 1.3 %copy-done = bf16[160,4096]{1,0:T(8,128)(2,1)S(1)} copy-done((bf16[160,4096]{1,0:T(8,128)(2,1)S(1)}, bf16[160,4096]{1,0:T(8,128)(2,1)}, u32[]{:S(2)}) %copy-start) | copy-done | bytes 1310744
  1.3 0.0 copy-start.1
  1.3 0.9 %copy-done.1 = bf16[160,512]{1,0:T(8,128)(2,1)S(1)} copy-done((bf16[160,512]{1,0:T(8,128)(2,1)S(1)}, bf16[160,512]{1,0:T(8,128)(2,1)}, u32[]{:S(2)}) %copy-start.1) | copy-done | bytes 163864
  2.2 0.0 copy-start.2
  2.2 0.9 %copy-done.2 = bf16[160,512]{1,0:T(8,128)(2,1)S(1)} copy-done((bf16[160,512]{1,0:T(8,128)(2,1)S(1)}, bf16[160,512]{1,0:T(8,128)(2,1)}, u32[]{:S(2)}) %copy-start.2) | copy-done | bytes 163864
  3.1 0.0 copy-start.3
  3.2 0.7 %copy-done.3 = f32[32]{0:T(128)S(1)} copy-done((f32[32]{0:T(128)S(1)}, f32[32]{0:T(128)}, u32[]{:S(2)}) %copy-start.3) | copy-done | bytes 152
  3.8 0.0 copy-start.4
  3.8 0.7 %copy-done.4 = s32[16]{0:T(128)S(1)} copy-done((s32[16]{0:T(128)S(1)}, s32[16]{0:T(128)}, u32[]{:S(2)}) %copy-start.4) | copy-done | bytes 88
  4.5 28.2 %shard_map.55 = bf16[160,4096]{1,0:T(8,128)(2,1)S(1)} custom-call(f32[32]{0:T(128)S(1)} %copy-done.3, s32[16]{0:T(128)S(1)} %copy-done.4, bf16[160,4096]{1,0:T(8,128)(2,1)S(1)} %copy-done, bf16[160,512]{1,0:T(8,128)(2,1)S(1)} %copy-done.1, bf16[160,512]{1,0:T(8,128)(2,1)S(1)} %copy-done.2), custom_call_target="tpu_custom_call" | custom-call | flops 2097152000 | bytes 2621440 | tf_op jit(solution)/shard_map/pallas_call | solution.py:264
  32.6 1.1 %copy.7 = bf16[160,4096]{1,0:T(8,128)(2,1)} copy(bf16[160,4096]{1,0:T(8,128)(2,1)S(1)} %shard_map.55) | data formatting | bytes 2621440
Async XLA Ops:
  0.0 1.3 %copy-start = (bf16[160,4096]{1,0:T(8,128)(2,1)S(1)}, bf16[160,4096]{1,0:T(8,128)(2,1)}, u32[]{:S(2)}) copy-start(bf16[160,4096]{1,0:T(8,128)(2,1)} %q_ref.1) | copy-start | bytes 3932164
  1.3 0.9 %copy-start.1 = (bf16[160,512]{1,0:T(8,128)(2,1)S(1)}, bf16[160,512]{1,0:T(8,128)(2,1)}, u32[]{:S(2)}) copy-start(bf16[160,512]{1,0:T(8,128)(2,1)} %k_ref.1) | copy-start | bytes 491524
  2.2 0.9 %copy-start.2 = (bf16[160,512]{1,0:T(8,128)(2,1)S(1)}, bf16[160,512]{1,0:T(8,128)(2,1)}, u32[]{:S(2)}) copy-start(bf16[160,512]{1,0:T(8,128)(2,1)} %v_ref.1) | copy-start | bytes 491524
  3.1 0.7 %copy-start.3 = (f32[32]{0:T(128)S(1)}, f32[32]{0:T(128)}, u32[]{:S(2)}) copy-start(f32[32]{0:T(128)} %scale_ref.1) | copy-start | bytes 388
  3.8 0.7 %copy-start.4 = (s32[16]{0:T(128)S(1)}, s32[16]{0:T(128)}, u32[]{:S(2)}) copy-start(s32[16]{0:T(128)} %len_ref.1) | copy-start | bytes 196

commit v2 on v1

--- a/solution.py
+++ b/solution.py
@@ -20,10 +20,26 @@
 
 
 def kernel(
-    n_ctx, n_grp, scale_ref, len_ref, q_ref, k_ref, v_ref, o_ref,
-    kw, vw, bias_own, bias_win, lv, acc, top, send_sem, recv_sem,
+    n_ctx, n_grp, scale_hbm, len_hbm, q_hbm, k_hbm, v_hbm, o_ref,
+    scale_ref, len_ref, q_ref, k_ref, v_ref,
+    kw, vw, bias, reach, live, lv, acc, top, load_sem, send_sem, recv_sem,
 ):
     rows = q_ref.shape[0]
+    loads = [
+        pltpu.make_async_copy(src, dst, load_sem.at[i])
+        for i, (src, dst) in enumerate(
+            (
+                (len_hbm, len_ref),
+                (scale_hbm, scale_ref),
+                (k_hbm, k_ref),
+                (v_hbm, v_ref),
+                (q_hbm, q_ref),
+            )
+        )
+    ]
+    for copy in loads:
+        copy.start()
+    small, large = loads[:2], loads[2:]
     n_dev = n_ctx * n_grp
     c = lax.axis_index("ctx")
     g = lax.axis_index("grp")
@@ -86,7 +102,7 @@
     def copies(src_slot, dst_slot, kind, half, dev):
         cols = pl.ds(half * HALF, HALF)
         made = []
-        for i, (own, win) in enumerate(((k_ref, kw), (v_ref, vw))):
+        for i, (own, win) in enumerate(((k_hbm, kw), (v_hbm, vw))):
             src = own.at[:, cols] if src_slot is None else win.at[src_slot, :, cols]
             made.append(
                 pltpu.make_async_remote_copy(
@@ -167,7 +183,10 @@
         def _():
             start(2, 3, 3, half, sibling)
 
-    pos = me * rows + lax.broadcasted_iota(jnp.int32, (rows, HD), 0)
+    for copy in small:
+        copy.wait()
+    first = me * rows
+    pos = first + lax.broadcasted_iota(jnp.int32, (rows, HD), 0)
 
     def doc(j, carry):
         total, begin = carry
@@ -178,58 +197,74 @@
     visible = pos - begin + 1
     factor = jnp.log(visible.astype(jnp.float32)) * (math.log2(math.e) / math.sqrt(HD))
     lv[...] = jnp.where(visible == 1, 1.0, factor)
-    for ref, base in ((bias_own, me * rows), (bias_win, (me - WIN_DEV) * rows)):
-        shape = ref.shape
-        k_pos = base + lax.broadcasted_iota(jnp.int32, shape, 1)
-        q_pos = me * rows + lax.broadcasted_iota(jnp.int32, shape, 0)
-        live = (k_pos >= jnp.broadcast_to(begin[:, :1], shape)) & (k_pos <= q_pos)
-        ref[...] = jnp.where(live, 0.0, MASKED)
+    k_pos = first + lax.broadcasted_iota(jnp.int32, (rows, rows), 1)
+    q_pos = first + lax.broadcasted_iota(jnp.int32, (rows, rows), 0)
+    seen = (k_pos >= jnp.broadcast_to(begin[:, :1], (rows, rows))) & (k_pos <= q_pos)
+    bias[...] = jnp.where(seen, 0.0, MASKED)
+    reach[...] = jnp.where(begin < first, 1.0, 0.0)
+    w_rows = WIN_DEV * rows
+    w_pos = first - w_rows + lax.broadcasted_iota(jnp.int32, (w_rows, HD), 0)
+    live[...] = jnp.where(w_pos >= begin[:1], 1.0, 0.0)
+    for copy in large:
+        copy.wait()
 
     def head_cols(h):
         return pl.ds(pl.multiple_of(h * HD, HD), HD)
 
-    def stacked(kv):
-        q = jnp.concatenate([q_ref[:, head_cols(kv * PER + i)] for i in range(PER)], axis=0)
-        fac = jnp.concatenate([lv[...] * scale_ref[kv * PER + i] for i in range(PER)], axis=0)
-        return q, fac[:, :1]
-
-    def scores(q, keys, bias):
-        s = lax.dot_general(q, keys, (((1,), (1,)), ((), ())), preferred_element_type=jnp.float32)
-        s = s.reshape(PER, rows, bias.shape[1]) + bias[...][None]
-        return s.reshape(PER * rows, bias.shape[1])
+    def scores(q, keys):
+        return lax.dot_general(q, keys, (((1,), (1,)), ((), ())), preferred_element_type=jnp.float32)
+
+    def spread(x, width):
+        whole = [x] * (width // HD)
+        if width % HD:
+            whole.append(x[:, : width % HD])
+        return jnp.concatenate(whole, axis=1)
 
     def mix(p, vals):
-        wide = jnp.concatenate([vals, jnp.ones(vals.shape, vals.dtype)], axis=1)
-        return jnp.dot(p.astype(jnp.bfloat16), wide, preferred_element_type=jnp.float32)
+        return jnp.dot(p.astype(jnp.bfloat16), vals, preferred_element_type=jnp.float32)
 
     def own_part(kv, _):
-        q, fac = stacked(kv)
-        s = scores(q, k_ref[:, head_cols(kv)], bias_own)
-        m = jnp.max(s, axis=1, keepdims=True)
-        acc[kv] = mix(jnp.exp2((s - m) * fac), v_ref[:, head_cols(kv)])
-        top[kv] = jnp.broadcast_to(m, top.shape[1:])
+        keys = k_ref[:, head_cols(kv)]
+        vals = v_ref[:, head_cols(kv)]
+        vals = jnp.concatenate([vals, jnp.ones(vals.shape, vals.dtype)], axis=1)
+        for i in range(PER):
+            h = kv * PER + i
+            fac = spread(lv[...] * scale_ref[h], rows)
+            s = scores(q_ref[:, head_cols(h)], keys) + bias[...]
+            m = jnp.max(s, axis=1, keepdims=True)
+            acc[h] = mix(jnp.exp2((s - m) * fac), vals)
+            top[h] = jnp.broadcast_to(m, top.shape[1:])
         return 0
 
     def window_part(kv, _):
-        q, fac = stacked(kv)
-        keys = kw[:, :, head_cols(kv)].reshape(WIN_DEV * rows, HD)
-        vals = vw[:, :, head_cols(kv)].reshape(WIN_DEV * rows, HD)
-        s = scores(q, keys, bias_win)
-        m_own = top[kv][:, :1]
-        m = jnp.maximum(m_own, jnp.max(s, axis=1, keepdims=True))
-        part = mix(jnp.exp2((s - m) * fac), vals)
-        both = acc[kv] * jnp.exp2((m_own - m) * fac) + part
-        out = (both[:, :HD] / both[:, HD:]).astype(o_ref.dtype)
+        alive = live[...]
+        keys = kw[:, :, head_cols(kv)].reshape(w_rows, HD).astype(jnp.float32)
+        keys = jnp.where(alive > 0, keys, k_ref[:16, head_cols(kv)].astype(jnp.float32)[:1])
+        keys = keys.astype(jnp.bfloat16)
+        vals = vw[:, :, head_cols(kv)].reshape(w_rows, HD).astype(jnp.float32)
+        vals = jnp.concatenate([jnp.where(alive > 0, vals, 0.0), alive], axis=1).astype(jnp.bfloat16)
+        reached = reach[...] > 0
+        both_reached = spread(reach[...], 2 * HD) > 0
         for i in range(PER):
-            o_ref[:, head_cols(kv * PER + i)] = out[i * rows : (i + 1) * rows]
+            h = kv * PER + i
+            fac = lv[...] * scale_ref[h]
+            s = scores(q_ref[:, head_cols(h)], keys)
+            m_own = top[h]
+            m_win = jnp.broadcast_to(jnp.max(s, axis=1, keepdims=True), m_own.shape)
+            m = jnp.where(reached, jnp.maximum(m_own, m_win), m_own)
+            part = mix(jnp.exp2((s - spread(m, w_rows)) * spread(fac, w_rows)), vals)
+            kept = spread(jnp.exp2((m_own - m) * fac), 2 * HD)
+            both = acc[h] * kept + jnp.where(both_reached, part, 0.0)
+            o_ref[:, head_cols(h)] = (both[:, :HD] / both[:, HD:]).astype(o_ref.dtype)
         return 0
 
     per_half = HK // HALVES
-    lax.fori_loop(0, per_half, own_part, 0)
+    lax.fori_loop(0, 2, own_part, 0)
     pass_on_far(0)
-    lax.fori_loop(per_half, HK, own_part, 0)
+    lax.fori_loop(2, 3, own_part, 0)
     pass_on_near(0)
     pass_on_far(1)
+    lax.fori_loop(3, 4, own_part, 0)
     pass_on_near(1)
     for half in range(HALVES):
         arrived(1, half)
@@ -258,27 +293,34 @@
     rows = queries.shape[0]
     n_ctx, n_grp = lax.axis_size("ctx"), lax.axis_size("grp")
     vmem = pl.BlockSpec(memory_space=pltpu.VMEM)
-    smem = pl.BlockSpec(memory_space=pltpu.SMEM)
+    hbm = pl.BlockSpec(memory_space=pltpu.HBM)
     window = pltpu.VMEM((WIN_DEV, rows, HK * HD), jnp.bfloat16)
     pairs = HQ * rows * (WIN_DEV + 1) * rows
     return pl.pallas_call(
         functools.partial(kernel, n_ctx, n_grp),
         out_shape=jax.ShapeDtypeStruct(queries.shape, queries.dtype),
-        in_specs=[smem, smem, vmem, vmem, vmem],
+        in_specs=[hbm] * 5,
         out_specs=vmem,
         scratch_shapes=[
+            pltpu.SMEM(ssmax_scale.shape, ssmax_scale.dtype),
+            pltpu.SMEM(lengths.shape, lengths.dtype),
+            pltpu.VMEM(queries.shape, queries.dtype),
+            pltpu.VMEM(keys.shape, keys.dtype),
+            pltpu.VMEM(values.shape, values.dtype),
             window,
             window,
             pltpu.VMEM((rows, rows), jnp.float32),
-            pltpu.VMEM((rows, WIN_DEV * rows), jnp.float32),
             pltpu.VMEM((rows, HD), jnp.float32),
-            pltpu.VMEM((HK, PER * rows, 2 * HD), jnp.float32),
-            pltpu.VMEM((HK, PER * rows, HD), jnp.float32),
+            pltpu.VMEM((WIN_DEV * rows, HD), jnp.float32),
+            pltpu.VMEM((rows, HD), jnp.float32),
+            pltpu.VMEM((HQ, rows, 2 * HD), jnp.float32),
+            pltpu.VMEM((HQ, rows, HD), jnp.float32),
+            pltpu.SemaphoreType.DMA((5,)),
             pltpu.SemaphoreType.DMA((4, HALVES, 2)),
             pltpu.SemaphoreType.DMA((4, HALVES, 2)),
         ],
         compiler_params=pltpu.CompilerParams(
-            collective_id=0, has_side_effects=True, vmem_limit_bytes=48 * 1024 * 1024
+            collective_id=0, has_side_effects=True, vmem_limit_bytes=63 * 1024 * 1024
         ),
         cost_estimate=pl.CostEstimate(
             flops=4 * pairs * HD, bytes_accessed=4 * queries.size, transcendentals=pairs

time: 33.9 us -> 28.9 us (0.85)
  local copies, waits for them, and re-layouts: 5.51 us -> 2.49 us
  Pallas kernels: 28.2 us -> 26.2 us
    unnamed x11 -> x1, local copies, waits for them, and re-layouts: 5.51 us -> 2.49 us
    pallas_call x1, Pallas kernels: 28.2 us -> 26.2 us  [body(): pl.pallas_call(functools.partial(kernel, n_ctx, n_grp), out_shape=jax.Sha...]
where the time goes in v2:
time: 28.9 us; the launch traced here: 28.7 us
  Pallas kernels  26.2 us (91%)
  local copies, waits for them, and re-layouts  2.49 us (9%)
    pallas_call x1, Pallas kernels, body(): pl.pallas_call(functools.partial(kernel, n_ctx, n_grp), out_shape=jax.Sha...  26.2 us
    unnamed x1, local copies, waits for them, and re-layouts  2.49 us

profile of v2, /device:TPU:24, one launch (start us, length us, event | category | flops | bytes accessed | tf_op | source)
XLA Modules:
  0.0 28.7 jit_solution(8554647610072841322)
XLA Ops:
  0.0 26.2 %shard_map.55 = bf16[160,4096]{1,0:T(8,128)(2,1)} custom-call(f32[32]{0:T(128)} %scale_hbm.1, s32[16]{0:T(128)} %len_hbm.1, bf16[160,4096]{1,0:T(8,128)(2,1)} %q_hbm.1, bf16[160,512]{1,0:T(8,128)(2,1)} %k_hbm.1, bf16[160,512]{1,0:T(8,128)(2,1)} %v_hbm.1), custom_call_target="tpu_custom_call" | custom-call | flops 2097152000 | bytes 2621440 | tf_op jit(solution)/shard_map/pallas_call | solution.py:299
  26.2 2.5 %copy.7 = bf16[160,4096]{1,0:T(8,128)(2,1)} copy(bf16[160,4096]{1,0:T(8,128)(2,1)} %shard_map.55) | data formatting | bytes 2621440

commit v3 on v2

--- a/solution.py
+++ b/solution.py
@@ -13,8 +13,7 @@
 HD = 128
 WIN_DEV = 4
 PER = HQ // HK
-HALVES = 2
-HALF = HK * HD // HALVES
+GROUP = 4
 MESH = pl.DeviceIdType.MESH
 MASKED = -1e30
 
@@ -99,8 +98,8 @@
 
     pl.semaphore_wait(barrier, count)
 
-    def copies(src_slot, dst_slot, kind, half, dev):
-        cols = pl.ds(half * HALF, HALF)
+    def copies(src_slot, dst_slot, kind, part, dev):
+        cols = pl.ds(part * HD, HD)
         made = []
         for i, (own, win) in enumerate(((k_hbm, kw), (v_hbm, vw))):
             src = own.at[:, cols] if src_slot is None else win.at[src_slot, :, cols]
@@ -108,8 +107,8 @@
                 pltpu.make_async_remote_copy(
                     src_ref=src,
                     dst_ref=win.at[dst_slot, :, cols],
-                    send_sem=send_sem.at[kind, half, i],
-                    recv_sem=recv_sem.at[dst_slot, half, i],
+                    send_sem=send_sem.at[kind, part, i],
+                    recv_sem=recv_sem.at[dst_slot, part, i],
                     device_id=dev,
                     device_id_type=MESH,
                 )
@@ -120,68 +119,68 @@
         for copy in copies(*args):
             copy.start()
 
-    def arrived(slot, half):
-        for copy in copies(None, slot, 0, half, sibling):
+    def arrived(slot, part):
+        for copy in copies(None, slot, 0, part, sibling):
             copy.wait_recv()
 
-    def sent(kind, half):
-        for copy in copies(None, 0, kind, half, sibling):
+    def sent(kind, part):
+        for copy in copies(None, 0, kind, part, sibling):
             copy.wait_send()
 
     first_chip = g < 2
-    for half in range(HALVES):
+    for part in range(HK):
 
         @pl.when(to4)
-        def _(half=half):
-            start(None, 0, 0, half, at(me + 4))
+        def _(part=part):
+            start(None, 0, 0, part, at(me + 4))
 
         if relay:
 
             @pl.when(first_chip)
-            def _(half=half):
-                start(None, 2, 1, half, across)
+            def _(part=part):
+                start(None, 2, 1, part, across)
 
         else:
 
             @pl.when(to2)
-            def _(half=half):
-                start(None, 2, 1, half, at(me + 2))
+            def _(part=part):
+                start(None, 2, 1, part, at(me + 2))
 
         @pl.when(core == 0)
-        def _(half=half):
-            start(None, 3, 2, half, sibling)
-
-    def pass_on_far(half):
+        def _(part=part):
+            start(None, 3, 2, part, sibling)
+
+    def pass_on_far(part):
         @pl.when(has4)
         def _():
-            arrived(0, half)
+            arrived(0, part)
 
         if relay:
 
             @pl.when(jnp.logical_not(first_chip))
             def _():
-                start(0, 2, 1, half, across)
+                start(0, 2, 1, part, across)
 
         @pl.when(core == 1)
         def _():
-            start(0, 1, 2, half, sibling)
-
-    def pass_on_near(half):
+            start(0, 1, 2, part, sibling)
+
+    def pass_on_near(part):
         if relay:
-            arrived(2, half)
+            arrived(2, part)
         else:
 
             @pl.when(has2)
             def _():
-                arrived(2, half)
+                arrived(2, part)
 
         @pl.when(core == 0)
         def _():
-            start(2, 1, 3, half, sibling)
+            start(2, 1, 3, part, sibling)
 
         @pl.when(core == 1)
         def _():
-            start(2, 3, 3, half, sibling)
+            start(2, 3, 3, part, sibling)
 
     for copy in small:
         copy.wait()
@@ -209,7 +208,7 @@
         copy.wait()
 
     def head_cols(h):
-        return pl.ds(pl.multiple_of(h * HD, HD), HD)
+        return pl.ds(h * HD, HD)
 
     def scores(q, keys):
         return lax.dot_general(q, keys, (((1,), (1,)), ((), ())), preferred_element_type=jnp.float32)
@@ -223,70 +222,77 @@
     def mix(p, vals):
         return jnp.dot(p.astype(jnp.bfloat16), vals, preferred_element_type=jnp.float32)
 
-    def own_part(kv, _):
+    def stacked(t):
+        heads = [t * GROUP + j for j in range(GROUP)]
+        q = jnp.concatenate([q_ref[:, head_cols(h)] for h in heads], axis=0)
+        fac = jnp.concatenate([lv[...] * scale_ref[h] for h in heads], axis=0)
+        return q, fac
+
+    def own_part(kv):
         keys = k_ref[:, head_cols(kv)]
         vals = v_ref[:, head_cols(kv)]
         vals = jnp.concatenate([vals, jnp.ones(vals.shape, vals.dtype)], axis=1)
-        for i in range(PER):
-            h = kv * PER + i
-            fac = spread(lv[...] * scale_ref[h], rows)
-            s = scores(q_ref[:, head_cols(h)], keys) + bias[...]
+        for i in range(PER // GROUP):
+            t = kv * (PER // GROUP) + i
+            q, fac = stacked(t)
+            s = scores(q, keys).reshape(GROUP, rows, rows) + bias[...][None]
+            s = s.reshape(GROUP * rows, rows)
             m = jnp.max(s, axis=1, keepdims=True)
-            acc[h] = mix(jnp.exp2((s - m) * fac), vals)
-            top[h] = jnp.broadcast_to(m, top.shape[1:])
-        return 0
-
-    def window_part(kv, _):
+            acc[t] = mix(jnp.exp2((s - m) * spread(fac, rows)), vals)
+            top[t] = jnp.broadcast_to(m, top.shape[1:])
+
+    def window_part(kv):
         alive = live[...]
         keys = kw[:, :, head_cols(kv)].reshape(w_rows, HD).astype(jnp.float32)
         keys = jnp.where(alive > 0, keys, k_ref[:16, head_cols(kv)].astype(jnp.float32)[:1])
         keys = keys.astype(jnp.bfloat16)
         vals = vw[:, :, head_cols(kv)].reshape(w_rows, HD).astype(jnp.float32)
         vals = jnp.concatenate([jnp.where(alive > 0, vals, 0.0), alive], axis=1).astype(jnp.bfloat16)
-        reached = reach[...] > 0
-        both_reached = spread(reach[...], 2 * HD) > 0
-        for i in range(PER):
-            h = kv * PER + i
-            fac = lv[...] * scale_ref[h]
-            s = scores(q_ref[:, head_cols(h)], keys)
-            m_own = top[h]
+        reaching = jnp.concatenate([reach[...]] * GROUP, axis=0)
+        reached = reaching > 0
+        both_reached = spread(reaching, 2 * HD) > 0
+        for i in range(PER // GROUP):
+            t = kv * (PER // GROUP) + i
+            q, fac = stacked(t)
+            s = scores(q, keys)
+            m_own = top[t]
             m_win = jnp.broadcast_to(jnp.max(s, axis=1, keepdims=True), m_own.shape)
             m = jnp.where(reached, jnp.maximum(m_own, m_win), m_own)
-            part = mix(jnp.exp2((s - spread(m, w_rows)) * spread(fac, w_rows)), vals)
+            mixed = mix(jnp.exp2((s - spread(m, w_rows)) * spread(fac, w_rows)), vals)
             kept = spread(jnp.exp2((m_own - m) * fac), 2 * HD)
-            both = acc[h] * kept + jnp.where(both_reached, part, 0.0)
-            o_ref[:, head_cols(h)] = (both[:, :HD] / both[:, HD:]).astype(o_ref.dtype)
-        return 0
-
-    per_half = HK // HALVES
-    lax.fori_loop(0, 2, own_part, 0)
-    pass_on_far(0)
-    lax.fori_loop(2, 3, own_part, 0)
-    pass_on_near(0)
-    pass_on_far(1)
-    lax.fori_loop(3, 4, own_part, 0)
-    pass_on_near(1)
-    for half in range(HALVES):
-        arrived(1, half)
-        arrived(3, half)
-        lax.fori_loop(half * per_half, (half + 1) * per_half, window_part, 0)
-
-    for half in range(HALVES):
+            both = acc[t] * kept + jnp.where(both_reached, mixed, 0.0)
+            out = (both[:, :HD] / both[:, HD:]).astype(o_ref.dtype)
+            for j in range(GROUP):
+                o_ref[:, head_cols(t * GROUP + j)] = out[j * rows : (j + 1) * rows]
+
+    for step in range(HK):
+        own_part(step)
+        pass_on_far(step)
+        if step:
+            pass_on_near(step - 1)
+    for step in range(HK):
+        arrived(1, step)
+        arrived(3, step)
+        window_part(step)
+        if step == 0:
+            pass_on_near(HK - 1)
+
+    for part in range(HK):
 
         @pl.when(to4)
-        def _(half=half):
-            sent(0, half)
+        def _(part=part):
+            sent(0, part)
 
         if relay:
-            sent(1, half)
+            sent(1, part)
         else:
 
             @pl.when(to2)
-            def _(half=half):
-                sent(1, half)
-
-        sent(2, half)
-        sent(3, half)
+            def _(part=part):
+                sent(1, part)
+
+        sent(2, part)
+        sent(3, part)
 
 
 def body(queries, keys, values, lengths, ssmax_scale):
@@ -313,19 +319,19 @@
             pltpu.VMEM((rows, HD), jnp.float32),
             pltpu.VMEM((WIN_DEV * rows, HD), jnp.float32),
             pltpu.VMEM((rows, HD), jnp.float32),
-            pltpu.VMEM((HQ, rows, 2 * HD), jnp.float32),
-            pltpu.VMEM((HQ, rows, HD), jnp.float32),
+            pltpu.VMEM((HQ // GROUP, GROUP * rows, 2 * HD), jnp.float32),
+            pltpu.VMEM((HQ // GROUP, GROUP * rows, HD), jnp.float32),
             pltpu.SemaphoreType.DMA((5,)),
-            pltpu.SemaphoreType.DMA((4, HALVES, 2)),
-            pltpu.SemaphoreType.DMA((4, HALVES, 2)),
+            pltpu.SemaphoreType.DMA((4, HK, 2)),
+            pltpu.SemaphoreType.DMA((4, HK, 2)),
         ],
         compiler_params=pltpu.CompilerParams(
-            collective_id=0, has_side_effects=True, vmem_limit_bytes=63 * 1024 * 1024
+            collective_id=0, has_side_effects=True, vmem_limit_bytes=48 * 1024 * 1024
         ),
         cost_estimate=pl.CostEstimate(
             flops=4 * pairs * HD, bytes_accessed=4 * queries.size, transcendentals=pairs
         ),
-    )(ssmax_scale, lengths, queries, keys, values)
+    )(*[pltpu.with_memory_space_constraint(x, pltpu.HBM) for x in (ssmax_scale, lengths, queries, keys, values)])
 
 
 def solution(mesh):

time: 28.9 us -> 22.3 us (0.77)
  Pallas kernels: 26.2 us -> 21.1 us
  local copies, waits for them, and re-layouts: 2.49 us -> 1.06 us
    pallas_call x1, Pallas kernels: 26.2 us -> 21.1 us  [body(): pl.pallas_call(functools.partial(kernel, n_ctx, n_grp), out_shape=jax.Sha...]
    unnamed x1, local copies, waits for them, and re-layouts: 2.49 us -> 1.06 us
where the time goes in v3:
time: 22.3 us; the launch traced here: 22.2 us
  Pallas kernels  21.1 us (95%)
  local copies, waits for them, and re-layouts  1.06 us (5%)
    pallas_call x1, Pallas kernels, body(): pl.pallas_call(functools.partial(kernel, n_ctx, n_grp), out_shape=jax.Sha...  21.1 us
    unnamed x1, local copies, waits for them, and re-layouts  1.06 us

profile of v3, /device:TPU:24, one launch (start us, length us, event | category | flops | bytes accessed | tf_op | source)
XLA Modules:
  0.0 22.2 jit_solution(17956560768988935731)
XLA Ops:
  0.0 21.1 %shard_map.55 = bf16[160,4096]{1,0:T(8,128)(2,1)S(1)} custom-call(f32[32]{0:T(128)} %scale_hbm.1, s32[16]{0:T(128)} %len_hbm.1, bf16[160,4096]{1,0:T(8,128)(2,1)} %q_hbm.1, bf16[160,512]{1,0:T(8,128)(2,1)} %k_hbm.1, bf16[160,512]{1,0:T(8,128)(2,1)} %v_hbm.1), custom_call_target="tpu_custom_call" | custom-call | flops 2097152000 | bytes 2621440 | tf_op jit(solution)/shard_map/pallas_call | solution.py:305
  21.1 1.1 %copy.7 = bf16[160,4096]{1,0:T(8,128)(2,1)} copy(bf16[160,4096]{1,0:T(8,128)(2,1)S(1)} %shard_map.55) | data formatting | bytes 2621440

commit v4 on v3

--- a/solution.py
+++ b/solution.py
@@ -128,26 +128,38 @@
             copy.wait_send()
 
     first_chip = g < 2
-    for part in range(HK):
-
+    def launch(part):
         @pl.when(to4)
-        def _(part=part):
+        def _():
             start(None, 0, 0, part, at(me + 4))
 
         if relay:
 
             @pl.when(first_chip)
-            def _(part=part):
+            def _():
                 start(None, 2, 1, part, across)
 
         else:
 
             @pl.when(to2)
-            def _(part=part):
+            def _():
                 start(None, 2, 1, part, at(me + 2))
 
-        @pl.when(core == 0)
-        def _(part=part):
+    def settle(part):
+        @pl.when(to4)
+        def _():
+            sent(0, part)
+
+        @pl.when(first_chip if relay else to2)
+        def _():
+            sent(1, part)
+
+    for part in range(2):
+        launch(part)
+
+    @pl.when(core == 0)
+    def _():
+        for part in range(HK):
             start(None, 3, 2, part, sibling)
 
     def pass_on_far(part):
@@ -228,11 +240,11 @@
         fac = jnp.concatenate([lv[...] * scale_ref[h] for h in heads], axis=0)
         return q, fac
 
-    def own_part(kv):
+    def own_part(kv, tiles=range(PER // GROUP)):
         keys = k_ref[:, head_cols(kv)]
         vals = v_ref[:, head_cols(kv)]
         vals = jnp.concatenate([vals, jnp.ones(vals.shape, vals.dtype)], axis=1)
-        for i in range(PER // GROUP):
+        for i in tiles:
             t = kv * (PER // GROUP) + i
             q, fac = stacked(t)
             s = scores(q, keys).reshape(GROUP, rows, rows) + bias[...][None]
@@ -265,32 +277,41 @@
             for j in range(GROUP):
                 o_ref[:, head_cols(t * GROUP + j)] = out[j * rows : (j + 1) * rows]
 
-    for step in range(HK):
-        own_part(step)
-        pass_on_far(step)
-        if step:
-            pass_on_near(step - 1)
+    own_part(0)
+    settle(0)
+    launch(2)
+    pass_on_far(0)
+    own_part(1)
+    settle(1)
+    launch(3)
+    own_part(2, (0,))
+    pass_on_far(1)
+    own_part(2, (1,))
+    pass_on_near(0)
+    own_part(3, (0,))
+    pass_on_far(2)
+    own_part(3, (1,))
+    pass_on_near(1)
     for step in range(HK):
         arrived(1, step)
         arrived(3, step)
         window_part(step)
         if step == 0:
-            pass_on_near(HK - 1)
+            pass_on_near(2)
+            pass_on_far(3)
+        if step == 1:
+            pass_on_near(3)
+
+    settle(2)
+    settle(3)
+    if relay:
+
+        @pl.when(jnp.logical_not(first_chip))
+        def _():
+            for part in range(HK):
+                sent(1, part)
 
     for part in range(HK):
-
-        @pl.when(to4)
-        def _(part=part):
-            sent(0, part)
-
-        if relay:
-            sent(1, part)
-        else:
-
-            @pl.when(to2)
-            def _(part=part):
-                sent(1, part)
-
         sent(2, part)
         sent(3, part)
 

time: 22.3 us -> 21.2 us (0.951)
  Pallas kernels: 21.1 us -> 19.8 us
    pallas_call x1, Pallas kernels: 21.1 us -> 19.8 us  [body(): pl.pallas_call(functools.partial(kernel, n_ctx, n_grp), out_shape=jax.Sha...]
where the time goes in v4:
time: 21.2 us; the launch traced here: 20.9 us
  Pallas kernels  19.8 us (93%)
  local copies, waits for them, and re-layouts  1.06 us (5%)
    pallas_call x1, Pallas kernels, body(): pl.pallas_call(functools.partial(kernel, n_ctx, n_grp), out_shape=jax.Sha...  19.8 us
    unnamed x1, local copies, waits for them, and re-layouts  1.06 us

profile of v4, /device:TPU:24, one launch (start us, length us, event | category | flops | bytes accessed | tf_op | source)
XLA Modules:
  0.0 20.9 jit_solution(15930251210305447609)
XLA Ops:
  0.0 19.8 %shard_map.55 = bf16[160,4096]{1,0:T(8,128)(2,1)S(1)} custom-call(f32[32]{0:T(128)} %scale_hbm.1, s32[16]{0:T(128)} %len_hbm.1, bf16[160,4096]{1,0:T(8,128)(2,1)} %q_hbm.1, bf16[160,512]{1,0:T(8,128)(2,1)} %k_hbm.1, bf16[160,512]{1,0:T(8,128)(2,1)} %v_hbm.1), custom_call_target="tpu_custom_call" | custom-call | flops 2097152000 | bytes 2621440 | tf_op jit(solution)/shard_map/pallas_call | solution.py:326
  19.8 1.1 %copy.7 = bf16[160,4096]{1,0:T(8,128)(2,1)} copy(bf16[160,4096]{1,0:T(8,128)(2,1)S(1)} %shard_map.55) | data formatting | bytes 2621440

commit v5 on v4

--- a/solution.py
+++ b/solution.py
@@ -253,7 +253,7 @@
             acc[t] = mix(jnp.exp2((s - m) * spread(fac, rows)), vals)
             top[t] = jnp.broadcast_to(m, top.shape[1:])
 
-    def window_part(kv):
+    def window_part(kv, tiles=range(PER // GROUP)):
         alive = live[...]
         keys = kw[:, :, head_cols(kv)].reshape(w_rows, HD).astype(jnp.float32)
         keys = jnp.where(alive > 0, keys, k_ref[:16, head_cols(kv)].astype(jnp.float32)[:1])
@@ -263,7 +263,7 @@
         reaching = jnp.concatenate([reach[...]] * GROUP, axis=0)
         reached = reaching > 0
         both_reached = spread(reaching, 2 * HD) > 0
-        for i in range(PER // GROUP):
+        for i in tiles:
             t = kv * (PER // GROUP) + i
             q, fac = stacked(t)
             s = scores(q, keys)
@@ -277,30 +277,36 @@
             for j in range(GROUP):
                 o_ref[:, head_cols(t * GROUP + j)] = out[j * rows : (j + 1) * rows]
 
+    def ready(part):
+        arrived(1, part)
+        arrived(3, part)
+
     own_part(0)
     settle(0)
     launch(2)
     pass_on_far(0)
-    own_part(1)
+    own_part(1, (0,))
     settle(1)
     launch(3)
-    own_part(2, (0,))
+    own_part(1, (1,))
     pass_on_far(1)
-    own_part(2, (1,))
+    own_part(2)
     pass_on_near(0)
-    own_part(3, (0,))
     pass_on_far(2)
-    own_part(3, (1,))
+    own_part(3)
+    ready(0)
+    window_part(0, (0,))
+    pass_on_far(3)
     pass_on_near(1)
-    for step in range(HK):
-        arrived(1, step)
-        arrived(3, step)
+    window_part(0, (1,))
+    pass_on_near(2)
+    ready(1)
+    window_part(1, (0,))
+    pass_on_near(3)
+    window_part(1, (1,))
+    for step in range(2, HK):
+        ready(step)
         window_part(step)
-        if step == 0:
-            pass_on_near(2)
-            pass_on_far(3)
-        if step == 1:
-            pass_on_near(3)
 
     settle(2)
     settle(3)

time: 21.2 us -> 22.4 us (1.057)
  the two profiles are of different devices: /device:TPU:24 before, /device:TPU:25 now
where the time goes in v5:
time: 22.4 us; the launch traced here: 22.3 us
  Pallas kernels  21.2 us (95%)
  local copies, waits for them, and re-layouts  1.06 us (5%)
    pallas_call x1, Pallas kernels, body(): pl.pallas_call(functools.partial(kernel, n_ctx, n_grp), out_shape=jax.Sha...  21.2 us
    unnamed x1, local copies, waits for them, and re-layouts  1.06 us

profile of v5, /device:TPU:25, one launch (start us, length us, event | category | flops | bytes accessed | tf_op | source)
XLA Modules:
  0.0 22.3 jit_solution(11306405979057103678)
XLA Ops:
  0.0 21.2 %shard_map.55 = bf16[160,4096]{1,0:T(8,128)(2,1)S(1)} custom-call(f32[32]{0:T(128)} %scale_hbm.1, s32[16]{0:T(128)} %len_hbm.1, bf16[160,4096]{1,0:T(8,128)(2,1)} %q_hbm.1, bf16[160,512]{1,0:T(8,128)(2,1)} %k_hbm.1, bf16[160,512]{1,0:T(8,128)(2,1)} %v_hbm.1), custom_call_target="tpu_custom_call" | custom-call | flops 2097152000 | bytes 2621440 | tf_op jit(solution)/shard_map/pallas_call | solution.py:332
  21.2 1.1 %copy.7 = bf16[160,4096]{1,0:T(8,128)(2,1)} copy(bf16[160,4096]{1,0:T(8,128)(2,1)S(1)} %shard_map.55) | data formatting | bytes 2621440

commit v6 on v4

--- a/solution.py
+++ b/solution.py
@@ -215,7 +215,7 @@
     reach[...] = jnp.where(begin < first, 1.0, 0.0)
     w_rows = WIN_DEV * rows
     w_pos = first - w_rows + lax.broadcasted_iota(jnp.int32, (w_rows, HD), 0)
-    live[...] = jnp.where(w_pos >= begin[:1], 1.0, 0.0)
+    live[...] = jnp.where(w_pos >= begin[:1], 1.0, 0.0).astype(live.dtype)
     for copy in large:
         copy.wait()
 
@@ -255,11 +255,10 @@
 
     def window_part(kv):
         alive = live[...]
-        keys = kw[:, :, head_cols(kv)].reshape(w_rows, HD).astype(jnp.float32)
-        keys = jnp.where(alive > 0, keys, k_ref[:16, head_cols(kv)].astype(jnp.float32)[:1])
-        keys = keys.astype(jnp.bfloat16)
-        vals = vw[:, :, head_cols(kv)].reshape(w_rows, HD).astype(jnp.float32)
-        vals = jnp.concatenate([jnp.where(alive > 0, vals, 0.0), alive], axis=1).astype(jnp.bfloat16)
+        stand_in = k_ref[:16, head_cols(kv)][:1] * (1 - alive)
+        keys = kw[:, :, head_cols(kv)].reshape(w_rows, HD) * alive + stand_in
+        vals = vw[:, :, head_cols(kv)].reshape(w_rows, HD) * alive
+        vals = jnp.concatenate([vals, alive], axis=1)
         reaching = jnp.concatenate([reach[...]] * GROUP, axis=0)
         reached = reaching > 0
         both_reached = spread(reaching, 2 * HD) > 0
@@ -338,7 +337,7 @@
             window,
             pltpu.VMEM((rows, rows), jnp.float32),
             pltpu.VMEM((rows, HD), jnp.float32),
-            pltpu.VMEM((WIN_DEV * rows, HD), jnp.float32),
+            pltpu.VMEM((WIN_DEV * rows, HD), jnp.bfloat16),
             pltpu.VMEM((rows, HD), jnp.float32),
             pltpu.VMEM((HQ // GROUP, GROUP * rows, 2 * HD), jnp.float32),
             pltpu.VMEM((HQ // GROUP, GROUP * rows, HD), jnp.float32),

time: 21.2 us -> 21.2 us (level)
  no operation moved by 1% of the time
where the time goes in v6:
time: 21.2 us; the launch traced here: 20.8 us
  Pallas kernels  19.8 us (93%)
  local copies, waits for them, and re-layouts  1.06 us (5%)
    pallas_call x1, Pallas kernels, body(): pl.pallas_call(functools.partial(kernel, n_ctx, n_grp), out_shape=jax.Sha...  19.8 us
    unnamed x1, local copies, waits for them, and re-layouts  1.06 us

profile of v6, /device:TPU:24, one launch (start us, length us, event | category | flops | bytes accessed | tf_op | source)
XLA Modules:
  0.0 20.8 jit_solution(3369641050990126183)
XLA Ops:
  0.0 19.8 %shard_map.55 = bf16[160,4096]{1,0:T(8,128)(2,1)S(1)} custom-call(f32[32]{0:T(128)} %scale_hbm.1, s32[16]{0:T(128)} %len_hbm.1, bf16[160,4096]{1,0:T(8,128)(2,1)} %q_hbm.1, bf16[160,512]{1,0:T(8,128)(2,1)} %k_hbm.1, bf16[160,512]{1,0:T(8,128)(2,1)} %v_hbm.1), custom_call_target="tpu_custom_call" | custom-call | flops 2097152000 | bytes 2621440 | tf_op jit(solution)/shard_map/pallas_call | solution.py:325
  19.8 1.1 %copy.7 = bf16[160,4096]{1,0:T(8,128)(2,1)} copy(bf16[160,4096]{1,0:T(8,128)(2,1)S(1)} %shard_map.55) | data formatting | bytes 2621440

commit v7 on v6

--- a/solution.py
+++ b/solution.py
@@ -13,7 +13,7 @@
 HD = 128
 WIN_DEV = 4
 PER = HQ // HK
-GROUP = 4
+GROUP = 8
 MESH = pl.DeviceIdType.MESH
 MASKED = -1e30
 
@@ -283,13 +283,11 @@
     own_part(1)
     settle(1)
     launch(3)
-    own_part(2, (0,))
+    own_part(2)
     pass_on_far(1)
-    own_part(2, (1,))
     pass_on_near(0)
-    own_part(3, (0,))
+    own_part(3)
     pass_on_far(2)
-    own_part(3, (1,))
     pass_on_near(1)
     for step in range(HK):
         arrived(1, step)

time: 21.2 us -> 23.6 us (1.11)
  the two profiles are of different devices: /device:TPU:24 before, /device:TPU:0 now
where the time goes in v7:
time: 23.6 us; the launch traced here: 23.5 us
  Pallas kernels  22.4 us (95%)
  local copies, waits for them, and re-layouts  1.06 us (4%)
    pallas_call x1, Pallas kernels, body(): pl.pallas_call(functools.partial(kernel, n_ctx, n_grp), out_shape=jax.Sha...  22.4 us
    unnamed x1, local copies, waits for them, and re-layouts  1.06 us

profile of v7, /device:TPU:0, one launch (start us, length us, event | category | flops | bytes accessed | tf_op | source)
XLA Modules:
  0.0 23.5 jit_solution(13856343552016214956)
XLA Ops:
  0.0 22.4 %shard_map.55 = bf16[160,4096]{1,0:T(8,128)(2,1)S(1)} custom-call(f32[32]{0:T(128)} %scale_hbm.1, s32[16]{0:T(128)} %len_hbm.1, bf16[160,4096]{1,0:T(8,128)(2,1)} %q_hbm.1, bf16[160,512]{1,0:T(8,128)(2,1)} %k_hbm.1, bf16[160,512]{1,0:T(8,128)(2,1)} %v_hbm.1), custom_call_target="tpu_custom_call" | custom-call | flops 2097152000 | bytes 2621440 | tf_op jit(solution)/shard_map/pallas_call | solution.py:323
  22.4 1.1 %copy.7 = bf16[160,4096]{1,0:T(8,128)(2,1)} copy(bf16[160,4096]{1,0:T(8,128)(2,1)S(1)} %shard_map.55) | data formatting | bytes 2621440
